TPU v7x, 32 devices: a whole 2x2x4 slice. The times are simulated.
32 devices in a mesh: groups: 2 (over y), blk: 4 (over z), heads: 2 (over x), sub: 2 (over core).
Axes of the slice: x: 2, y: 2, z: 4, core: 2. Of those that a mesh axis runs over, the one named last changes fastest.
Arguments:
- patches: bfloat16 [1024, 1024], P(('groups', 'blk')), parts along dimension 0, may hold values from -6 to 6
- conv_taps: float32 [3, 1024], replicated, may hold values from -3 to 3
- w_query: bfloat16 [1024, 1024], P(None, ('heads', 'sub')), may hold values from -0.1875 to 0.1875
- w_key: bfloat16 [1024, 1024], P(None, ('heads', 'sub')), may hold values from -0.1875 to 0.1875
- w_value: bfloat16 [1024, 1024], P(None, ('heads', 'sub')), may hold values from -0.1875 to 0.1875
- w_output: bfloat16 [1024, 1024], P(None, ('heads', 'sub')), may hold values from -0.1875 to 0.1875
- tile_mask: int32 [8, 4], P('groups'), parts along dimension 0, may hold values from 0 to 1, as said below
- cotangent: bfloat16 [1024, 1024], P(('groups', 'blk'), ('heads', 'sub')), parts along dimension 0, may hold values from -6 to 6
Outputs:
- input_grad: float32 [1024, 1024], P(('groups', 'blk'), ('heads', 'sub')), parts along dimension 0
- conv_grad: float32 [6, 1024], P('groups', ('heads', 'sub')), parts along dimension 0
- grad_query: float32 [2048, 1024], P(('groups', 'blk'), ('heads', 'sub')), parts along dimension 0
- grad_key: float32 [2048, 1024], P(('groups', 'blk'), ('heads', 'sub')), parts along dimension 0
- grad_value: float32 [2048, 1024], P(('groups', 'blk'), ('heads', 'sub')), parts along dimension 0
- grad_output: float32 [2048, 1024], P(('groups', 'blk'), ('heads', 'sub')), parts along dimension 0
There are 2 independent parts, one for each index of `groups`. A program takes and returns all parts, laid end to end along the dimension named above; an argument that names none is the same for every part. Nothing has to cross between parts.
Inputs may be any that keep to these rules, and one draw needn't show every extreme that they name: tile_mask[i][i] is 1 for every tile and tile_mask is symmetric.
All inputs are finite; a program needn't handle non-finite values.
Results may differ from a plain program's by a relative error of at most 0.004.
The roundings to bfloat16 on the way count: a program that leaves them out, or rounds other values in their place, can miss the bound.
Values may be sent and summed in bfloat16 or wider, within the bound.
A program may use at most 64 MiB of HBM per device.

v0:
```python
import jax
import jax.numpy as jnp
from jax import lax
from jax.sharding import PartitionSpec as P

D = 1024
HEADS = 16
TILE = 128


def padded(cells, sides, width):
    for axis, dim in sides:
        count = lax.axis_size(axis)
        ends = count - 1
        head = lax.slice_in_dim(cells, 0, width, axis=dim)
        tail = lax.slice_in_dim(cells, cells.shape[dim] - width, cells.shape[dim], axis=dim)
        cells = jnp.concatenate(
            [
                lax.ppermute(tail, axis, [(i, (i + 1) % count) for i in range(ends)]),
                cells,
                lax.ppermute(head, axis, [((i + 1) % count, i) for i in range(ends)]),
            ],
            axis=dim,
        )
    return cells


def from_behind(value, axis, steps):
    count = lax.axis_size(axis)
    pairs = [(source, (source + steps) % count) for source in range(count)]
    return lax.ppermute(value, axis, pairs)


def allowed_rows(mask_bf, first_query, query_count, first_key, key_count):
    tiles = mask_bf.shape[0]
    columns = jnp.arange(tiles, dtype=jnp.int32)
    query_tiles = (first_query + jnp.arange(query_count, dtype=jnp.int32)) // TILE
    key_tiles = (first_key + jnp.arange(key_count, dtype=jnp.int32)) // TILE
    query_hot = (query_tiles[:, None] == columns[None, :]).astype(jnp.bfloat16)
    key_hot = (key_tiles[:, None] == columns[None, :]).astype(jnp.bfloat16)
    picked = jnp.dot(query_hot, mask_bf, preferred_element_type=jnp.float32).astype(jnp.bfloat16)
    return jnp.einsum("qn,kn->qk", picked, key_hot, preferred_element_type=jnp.float32) > 0.5


def per_device(patches, conv_taps, w_query, w_key, w_value, w_output, tile_mask, cotangent):
    rows = patches.shape[0]
    local = w_query.shape[1]
    head_size = D // HEADS
    heads_here = local // head_size
    cycle_size = lax.axis_size("blk")
    position = lax.axis_index("blk")
    total_rows = rows * cycle_size
    scale = head_size ** (-0.5)
    norm = total_rows ** (-0.5)
    mask_bf = tile_mask.astype(jnp.bfloat16)
    first_query = position * rows
    padded_in = padded(patches, (("blk", 0),), 1)
    padded32 = padded_in.astype(jnp.float32)
    middle = padded32[1:-1]
    mixed = (
        middle + conv_taps[0] * padded32[:-2] + conv_taps[1] * middle + conv_taps[2] * padded32[2:]
    ).astype(jnp.bfloat16)
    queries = jnp.dot(mixed, w_query, preferred_element_type=jnp.float32).astype(jnp.bfloat16)
    keys_own = jnp.dot(mixed, w_key, preferred_element_type=jnp.float32).astype(jnp.bfloat16)
    values_own = jnp.dot(mixed, w_value, preferred_element_type=jnp.float32).astype(jnp.bfloat16)
    keys_all, values_all = (
        lax.all_gather(keys_own, "blk", axis=0, tiled=True),
        lax.all_gather(values_own, "blk", axis=0, tiled=True),
    )
    cot_full = lax.all_gather(cotangent, ("heads", "sub"), axis=1, tiled=True)
    grad_att = jnp.dot(cot_full, w_output, preferred_element_type=jnp.float32).astype(jnp.bfloat16)
    group = 1
    for power in range(12):
        if group * 2 * rows <= 1024 and cycle_size % (group * 2) == 0:
            group = group * 2
    span = group * rows
    blocks = cycle_size // group
    query_heads = queries.reshape(rows, heads_here, head_size)
    grad_heads = grad_att.reshape(rows, heads_here, head_size)
    key_blocks = keys_all.reshape(blocks, span, heads_here, head_size)
    value_blocks = values_all.reshape(blocks, span, heads_here, head_size)
    block_ids = jnp.arange(blocks, dtype=jnp.int32)

    def weights_of(key_block, allowed):
        raw = (
            jnp.einsum("qhd,khd->hqk", query_heads, key_block, preferred_element_type=jnp.float32)
            * scale
        )
        return jnp.where(allowed[None], jnp.exp(jnp.where(allowed[None], raw, 0.0)), 0.0)

    def forward_step(state, inputs):
        block_id, key_block, value_block = inputs
        allowed = allowed_rows(mask_bf, first_query, rows, block_id * span, span)
        accum, totals = state
        weights = weights_of(key_block, allowed)
        added = jnp.einsum(
            "hqk,khd->hqd",
            weights.astype(jnp.bfloat16),
            value_block,
            preferred_element_type=jnp.float32,
        )
        state = (accum + added, totals + jnp.sum(weights, -1))
        return (state, None)

    start_state = (
        jnp.zeros((heads_here, rows, head_size), jnp.float32),
        jnp.zeros((heads_here, rows), jnp.float32),
    )
    (accum, totals), unused = lax.scan(
        forward_step, start_state, (block_ids, key_blocks, value_blocks)
    )
    attended32 = accum / totals[:, :, None]
    attended = jnp.transpose(attended32, (1, 0, 2)).reshape(rows, local).astype(jnp.bfloat16)
    deltas = jnp.einsum("qhd,hqd->hq", grad_heads.astype(jnp.float32), attended32)

    def local_grads(key_block, value_block, allowed):
        weights = weights_of(key_block, allowed)
        probs = weights / totals[:, :, None]
        dprobs = jnp.einsum(
            "qhd,khd->hqk", grad_heads, value_block, preferred_element_type=jnp.float32
        )
        dscores = (probs * (dprobs - deltas[:, :, None]) * scale).astype(jnp.bfloat16)
        return (
            jnp.einsum("hqk,khd->qhd", dscores, key_block, preferred_element_type=jnp.float32),
            jnp.einsum("hqk,qhd->khd", dscores, query_heads, preferred_element_type=jnp.float32),
            jnp.einsum(
                "hqk,qhd->khd",
                probs.astype(jnp.bfloat16),
                grad_heads,
                preferred_element_type=jnp.float32,
            ),
        )

    def shard_grads(block):
        wrapped = jnp.remainder(block, cycle_size)
        key_block = lax.dynamic_slice_in_dim(keys_all, wrapped * rows, rows, 0).reshape(
            rows, heads_here, head_size
        )
        value_block = lax.dynamic_slice_in_dim(values_all, wrapped * rows, rows, 0).reshape(
            rows, heads_here, head_size
        )
        allowed = allowed_rows(mask_bf, first_query, rows, wrapped * rows, rows)
        query_add, key_term, value_term = local_grads(key_block, value_block, allowed)
        return (
            query_add,
            jnp.stack([key_term.reshape(rows, local), value_term.reshape(rows, local)]),
        )

    query_first, carried_first = shard_grads(position - 1)

    def turn(step, state):
        accum_q, carried = state
        moved = from_behind(carried, "blk", 1)
        query_add, term = shard_grads(position - step - 1)
        return (accum_q + query_add, moved + term)

    accum_q, summed = lax.fori_loop(1, cycle_size, turn, (query_first, carried_first))
    grad_keys = summed[0].astype(jnp.bfloat16)
    grad_values = summed[1].astype(jnp.bfloat16)
    grad_queries = accum_q.reshape(rows, local).astype(jnp.bfloat16)
    stacked = jnp.stack(
        [
            jnp.einsum("td,tc->dc", mixed, grad_queries, preferred_element_type=jnp.float32),
            jnp.einsum("td,tc->dc", mixed, grad_keys, preferred_element_type=jnp.float32),
            jnp.einsum("td,tc->dc", mixed, grad_values, preferred_element_type=jnp.float32),
            jnp.einsum("td,tc->dc", cot_full, attended, preferred_element_type=jnp.float32),
        ]
    )
    weight_sums = lax.psum_scatter(stacked, "blk", scatter_dimension=1, tiled=True) * norm
    partial_grad = (
        jnp.einsum("tc,dc->td", grad_queries, w_query, preferred_element_type=jnp.float32)
        + jnp.einsum("tc,dc->td", grad_keys, w_key, preferred_element_type=jnp.float32)
        + jnp.einsum("tc,dc->td", grad_values, w_value, preferred_element_type=jnp.float32)
    )
    grad_mixed = lax.psum_scatter(
        partial_grad, ("heads", "sub"), scatter_dimension=1, tiled=True
    ) + cotangent.astype(jnp.float32)
    columns_here = cotangent.shape[1]
    offset = lax.axis_index(("heads", "sub")) * columns_here
    taps_here = lax.dynamic_slice_in_dim(conv_taps, offset, columns_here, 1)
    padded_grad = padded(grad_mixed.astype(jnp.bfloat16), (("blk", 0),), 1).astype(grad_mixed.dtype)
    input_grad = (
        grad_mixed * (1.0 + taps_here[1])
        + taps_here[0] * padded_grad[2:]
        + taps_here[2] * padded_grad[:-2]
    )
    patch_cols = lax.dynamic_slice_in_dim(padded32, offset, columns_here, 1)
    conv_terms = jnp.stack(
        [
            jnp.sum(grad_mixed * patch_cols[:-2], 0),
            jnp.sum(grad_mixed * patch_cols[1:-1], 0),
            jnp.sum(grad_mixed * patch_cols[2:], 0),
        ]
    )
    conv_grad = lax.psum(conv_terms, "blk") * norm
    return (input_grad, conv_grad, weight_sums[0], weight_sums[1], weight_sums[2], weight_sums[3])


def solution(mesh):
    in_specs = (
        P(("groups", "blk"), None),
        P(),
        P(None, ("heads", "sub")),
        P(None, ("heads", "sub")),
        P(None, ("heads", "sub")),
        P(None, ("heads", "sub")),
        P("groups", None),
        P(("groups", "blk"), ("heads", "sub")),
    )
    out_specs = (
        P(("groups", "blk"), ("heads", "sub")),
        P("groups", ("heads", "sub")),
        P(("groups", "blk"), ("heads", "sub")),
        P(("groups", "blk"), ("heads", "sub")),
        P(("groups", "blk"), ("heads", "sub")),
        P(("groups", "blk"), ("heads", "sub")),
    )
    return jax.shard_map(
        per_device, mesh=mesh, in_specs=in_specs, out_specs=out_specs, check_vma=False
    )
```

profile of v0, /device:TPU:0, one launch (start us, length us, event | category | flops | bytes accessed | tf_op | source)
XLA Modules:
  0.0 201.9 jit_solution(833007776584470410)
XLA Ops:
  7.2 0.9 fusion.47
  8.1 4.9 %collective-permute-start.1 = (bf16[1,1024]{1,0:T(2,128)(2,1)S(1)}, bf16[1,1024]{1,0:T(2,128)(2,1)S(1)}, u32[]{:S(2)}, u32[]{:S(2)}) collective-permute-start(bf16[1,1024]{1,0:T(2,128)(2,1)S(1)} %get-tuple-element.416), channel_id=1, source_target_pairs={{0,4},{4,8},{8,12},{1,5},{5,9},{9,13},{2,6},{6,10},{10,14},{3,7},{... | collective-permute-start | bytes 6152 | tf_op jit(solution)/shard_map/ppermute | solution.py:19
  13.0 1.3 collective-permute-start.2
  15.9 6.0 %all_gather.10 = bf16[128,1024]{1,0:T(8,128)(2,1)S(1)} all-gather(bf16[128,256]{1,0:T(8,128)(2,1)} %param.17), channel_id=1, replica_groups=mesh['groups'=2,'blk'=4,'heads'=2,'sub'=2] {'heads','sub'}, dimensions={1}, use_global_device_ids=true | all-gather | bytes 327680 | tf_op jit(solution)/shard_map/all_gather | solution.py:70
  22.5 1.3 convolution_convert_fusion.2
  24.2 1.0 maximum_convert_fusion
  26.3 15.2 %all_gather.9 = bf16[512,256]{1,0:T(8,128)(2,1)S(1)} all-gather(bf16[128,256]{1,0:T(8,128)(2,1)S(1)} %convolution_convert_fusion.4), channel_id=1, replica_groups=mesh['groups'=2,'blk'=4,'heads'=2,'sub'=2] {'blk'}, dimensions={0}, use_global_device_ids=true | all-gather | bytes 327680 | tf_op jit(solution)/shard_map/all_gather | solution.py:67
  41.4 14.4 %all_gather.11 = bf16[512,256]{1,0:T(8,128)(2,1)S(1)} all-gather(bf16[128,256]{1,0:T(8,128)(2,1)S(1)} %convolution_convert_fusion.1), channel_id=1, replica_groups=mesh['groups'=2,'blk'=4,'heads'=2,'sub'=2] {'blk'}, dimensions={0}, use_global_device_ids=true | all-gather | bytes 327680 | tf_op jit(solution)/shard_map/all_gather | solution.py:68
  55.9 0.8 copy.38
  57.8 1.5 fusion.50
  59.6 1.9 fusion.37
  62.3 29.1 %while.23 = (s32[]{:T(128)}, f32[128,4,64]{0,2,1:T(8,128)S(1)}, f32[2,128,256]{1,2,0:T(8,128)S(1)}, s32[]{:T(128)}, bf16[512,256]{0,1:T(8,128)(2,1)}, /*index=5*...) while((s32[]{:T(128)}, f32[128,4,64]{0,2,1:T(8,128)S(1)}, ...), condition=%wide.region_2.3_spmd, body=%wide.region_1.2_spmd.sunk | while | flops 42853904 | bytes 4331956 | solution.py:157
  62.3 1.6 collective-permute-start
  64.5 0.9 constant_dynamic-slice_fusion.6
  66.5 5.7 %collective-permute-done = f32[2,128,256]{1,2,0:T(8,128)S(1)} collective-permute-done((f32[2,128,256]{1,2,0:T(8,128)S(1)}, f32[2,128,256]{1,2,0:T(8,128)S(1)}, u32[]{:S(2)}, u32[]{:S(2)}) %collective-permute-start) | collective-permute-done | bytes 262176 | tf_op jit(solution)/shard_map/while/body/eval_jaxpr/ppermute | solution.py:31
  72.2 1.0 collective-permute-start
  73.7 0.9 constant_dynamic-slice_fusion.6
  75.6 7.4 %collective-permute-done = f32[2,128,256]{1,2,0:T(8,128)S(1)} collective-permute-done((f32[2,128,256]{1,2,0:T(8,128)S(1)}, f32[2,128,256]{1,2,0:T(8,128)S(1)}, u32[]{:S(2)}, u32[]{:S(2)}) %collective-permute-start) | collective-permute-done | bytes 262176 | tf_op jit(solution)/shard_map/while/body/eval_jaxpr/ppermute | solution.py:31
  83.7 0.9 constant_dynamic-slice_fusion.6
  85.7 5.7 %collective-permute-done = f32[2,128,256]{1,2,0:T(8,128)S(1)} collective-permute-done((f32[2,128,256]{1,2,0:T(8,128)S(1)}, f32[2,128,256]{1,2,0:T(8,128)S(1)}, u32[]{:S(2)}, u32[]{:S(2)}) %collective-permute-start) | collective-permute-done | bytes 262176 | tf_op jit(solution)/shard_map/while/body/eval_jaxpr/ppermute | solution.py:31
  92.1 1.1 convolution_add_fusion
  94.6 2.2 %pad_maximum_fusion = f32[4,1024,256]{2,1,0:T(8,128)} fusion(f32[1,1024,256]{2,1,0:T(8,128)S(1)} %convolution_bitcast_fusion.1, f32[1,1024,256]{2,1,0:T(8,128)S(1)} %convolution_bitcast_fusion.2, f32[1,1024,256]{2,1,0:T(8,128)S(1)} %convolution_bitcast_fusion.3, f32[1,1024,256]{2,1,0:T(8,128)S(1)} %convolution_bitcast_fusion.4), kind=kLoop, calls=%fused_computation.32 | loop fusion | flops 3145728 | bytes 8388608 | tf_op jit(solution)/shard_map/stack | solution.py:161
  96.9 0.9 dynamic-slice_add_fusion
  97.8 15.5 %reduce-scatter.3.cloned.1.call-done = f32[128,256]{1,0:T(8,128)} async-done(((f32[128,1024]{1,0:T(8,128)}), f32[128,256]{1,0:T(8,128)}) %reduce-scatter.3.cloned.1.call-update) | async-done | bytes 131088 | tf_op jit(solution)/shard_map/reduce_scatter | solution.py:175
  113.3 1.1 fusion.33
  114.3 3.4 %collective-permute-start.3 = (bf16[1,256]{1,0:T(2,128)(2,1)S(1)}, bf16[1,256]{1,0:T(2,128)(2,1)S(1)}, u32[]{:S(2)}, u32[]{:S(2)}) collective-permute-start(bf16[1,256]{1,0:T(2,128)(2,1)S(1)} %get-tuple-element.419), channel_id=1, source_target_pairs={{0,4},{4,8},{8,12},{1,5},{5,9},{9,13},{2,6},{6,10},{10,14},{3,7},{... | collective-permute-start | bytes 1544 | tf_op jit(solution)/shard_map/ppermute | solution.py:19
  117.7 1.3 collective-permute-start.4
  119.1 13.3 %psum.7 = f32[3,256]{1,0:T(4,128)S(1)} all-reduce(f32[3,256]{1,0:T(4,128)S(1)} %pad_maximum_fusion.2), channel_id=1, replica_groups=mesh['groups'=2,'blk'=4,'heads'=2,'sub'=2] {'blk'}, use_global_device_ids=true, to_apply=%region_7.8 | all-reduce | flops 768 | bytes 6144 | tf_op jit(solution)/shard_map/psum | solution.py:195
  133.0 1.6 fusion.34
  134.6 58.2 %reduce-scatter.5.cloned.1.call-done = f32[4,256,256]{2,1,0:T(8,128)} async-done(((f32[4,1024,256]{2,1,0:T(8,128)}), f32[4,256,256]{2,1,0:T(8,128)}) %reduce-scatter.5.cloned.1.call-update) | async-done | bytes 1048592 | tf_op jit(solution)/shard_map/reduce_scatter | solution.py:169
  192.7 1.3 broadcast_multiply_fusion
  194.1 1.0 slice_bitcast_fusion
  (86 shorter events, 13.0 us)
Async XLA Ops:
  7.2 18.5 %copy-start = (bf16[1024,256]{1,0:T(8,128)(2,1)S(1)}, bf16[1024,256]{1,0:T(8,128)(2,1)}, u32[]{:S(2)}) copy-start(bf16[1024,256]{1,0:T(8,128)(2,1)} %param.12) | copy-start | bytes 1572868
  7.2 18.2 %copy-start.2 = (bf16[1024,256]{1,0:T(8,128)(2,1)S(1)}, bf16[1024,256]{1,0:T(8,128)(2,1)}, u32[]{:S(2)}) copy-start(bf16[1024,256]{1,0:T(8,128)(2,1)} %param.14) | copy-start | bytes 1572868
  7.2 18.8 %copy-start.1 = (bf16[1024,256]{1,0:T(8,128)(2,1)S(1)}, bf16[1024,256]{1,0:T(8,128)(2,1)}, u32[]{:S(2)}) copy-start(bf16[1024,256]{1,0:T(8,128)(2,1)} %param.13) | copy-start | bytes 1572868
  7.2 106.1 %reduce-scatter.3.cloned.1.call-start = ((), (), s32[]{:S(2)}) async-start(), calls=%async_computation.2 | async-start | bytes 655360 | tf_op jit(solution)/shard_map/reduce_scatter | solution.py:175
  8.1 16.1 %collective-permute-start.1 = (bf16[1,1024]{1,0:T(2,128)(2,1)S(1)}, bf16[1,1024]{1,0:T(2,128)(2,1)S(1)}, u32[]{:S(2)}, u32[]{:S(2)}) collective-permute-start(bf16[1,1024]{1,0:T(2,128)(2,1)S(1)} %get-tuple-element.416), channel_id=1, source_target_pairs={{0,4},{4,8},{8,12},{1,5},{5,9},{9,13},{2,6},{6,10},{10,14},{3,7},{... | collective-permute-start | bytes 6152 | tf_op jit(solution)/shard_map/ppermute | solution.py:19
  13.0 11.1 %collective-permute-start.2 = (bf16[1,1024]{1,0:T(2,128)(2,1)S(1)}, bf16[1,1024]{1,0:T(2,128)(2,1)S(1)}, u32[]{:S(2)}, u32[]{:S(2)}) collective-permute-start(bf16[1,1024]{1,0:T(2,128)(2,1)S(1)} %get-tuple-element.417), channel_id=1, source_target_pairs={{4,0},{8,4},{12,8},{5,1},{9,5},{13,9},{6,2},{10,6},{14,10},{7,3},{... | collective-permute-start | bytes 6152 | tf_op jit(solution)/shard_map/ppermute | solution.py:21
  62.3 9.8 %collective-permute-start = (f32[2,128,256]{1,2,0:T(8,128)S(1)}, f32[2,128,256]{1,2,0:T(8,128)S(1)}, u32[]{:S(2)}, u32[]{:S(2)}) collective-permute-start(f32[2,128,256]{1,2,0:T(8,128)S(1)} %get-tuple-element.533), channel_id=1, source_target_pairs={{0,4},{4,8},{8,12},{12,0},{1,5},{5,9},{9,13},{13,1},{2,6},{6,10},{... | collective-permute-start | bytes 786440 | tf_op jit(solution)/shard_map/while/body/eval_jaxpr/ppermute | solution.py:31
  72.2 10.9 %collective-permute-start = (f32[2,128,256]{1,2,0:T(8,128)S(1)}, f32[2,128,256]{1,2,0:T(8,128)S(1)}, u32[]{:S(2)}, u32[]{:S(2)}) collective-permute-start(f32[2,128,256]{1,2,0:T(8,128)S(1)} %get-tuple-element.533), channel_id=1, source_target_pairs={{0,4},{4,8},{8,12},{12,0},{1,5},{5,9},{9,13},{13,1},{2,6},{6,10},{... | collective-permute-start | bytes 786440 | tf_op jit(solution)/shard_map/while/body/eval_jaxpr/ppermute | solution.py:31
  83.1 8.2 %collective-permute-start = (f32[2,128,256]{1,2,0:T(8,128)S(1)}, f32[2,128,256]{1,2,0:T(8,128)S(1)}, u32[]{:S(2)}, u32[]{:S(2)}) collective-permute-start(f32[2,128,256]{1,2,0:T(8,128)S(1)} %get-tuple-element.533), channel_id=1, source_target_pairs={{0,4},{4,8},{8,12},{12,0},{1,5},{5,9},{9,13},{13,1},{2,6},{6,10},{... | collective-permute-start | bytes 786440 | tf_op jit(solution)/shard_map/while/body/eval_jaxpr/ppermute | solution.py:31
  91.7 2.5 %copy-start.4 = (f32[4,128,64]{1,2,0:T(8,128)S(1)}, f32[4,128,64]{1,2,0:T(8,128)}, u32[]{:S(2)}) copy-start(f32[4,128,64]{1,2,0:T(8,128)} %get-tuple-element.430) | copy-start | bytes 393220
  93.2 99.5 %reduce-scatter.5.cloned.1.call-start = ((), (), s32[]{:S(2)}) async-start(), calls=%async_computation.3 | async-start | bytes 5242880 | tf_op jit(solution)/shard_map/reduce_scatter | solution.py:169
  96.9 16.4 %copy-start.3 = (bf16[128,256]{1,0:T(8,128)(2,1)S(1)}, bf16[128,256]{1,0:T(8,128)(2,1)}, u32[]{:S(2)}) copy-start(bf16[128,256]{1,0:T(8,128)(2,1)} %param.17) | copy-start | bytes 196612
  114.3 18.6 %collective-permute-start.3 = (bf16[1,256]{1,0:T(2,128)(2,1)S(1)}, bf16[1,256]{1,0:T(2,128)(2,1)S(1)}, u32[]{:S(2)}, u32[]{:S(2)}) collective-permute-start(bf16[1,256]{1,0:T(2,128)(2,1)S(1)} %get-tuple-element.419), channel_id=1, source_target_pairs={{0,4},{4,8},{8,12},{1,5},{5,9},{9,13},{2,6},{6,10},{10,14},{3,7},{... | collective-permute-start | bytes 1544 | tf_op jit(solution)/shard_map/ppermute | solution.py:19
  117.7 15.2 %collective-permute-start.4 = (bf16[1,256]{1,0:T(2,128)(2,1)S(1)}, bf16[1,256]{1,0:T(2,128)(2,1)S(1)}, u32[]{:S(2)}, u32[]{:S(2)}) collective-permute-start(bf16[1,256]{1,0:T(2,128)(2,1)S(1)} %get-tuple-element.420), channel_id=1, source_target_pairs={{4,0},{8,4},{12,8},{5,1},{9,5},{13,9},{6,2},{10,6},{14,10},{7,3},{... | collective-permute-start | bytes 1544 | tf_op jit(solution)/shard_map/ppermute | solution.py:21
Sparse Core Ops, SparseCore 0:
  93.4 19.8 reduce-scatter.2
  115.7 77.0 reduce-scatter.4
where the time goes:
time: 203 us; the launch traced here: 202 us
  waiting for transfers between devices  92.5 us (46%)
  blocking collectives  48.9 us (24%)
  matrix products  14.4 us (7%)
  between operations  14.4 us (7%)
  starting transfers between devices  13.7 us (7%)
  other arithmetic  9.88 us (5%)
  local copies, waits for them, and re-layouts  7.87 us (4%)
    reduce_scatter x1, waiting for transfers between devices, per_device(): lax.psum_scatter(stacked, 'blk', scatter_dimension=1, tiled=True) * norm  58.2 us
    ppermute x3, waiting for transfers between devices, from_behind(): return lax.ppermute(value, axis, pairs)  18.8 us
    reduce_scatter x1, waiting for transfers between devices, per_device(): lax.psum_scatter(partial_grad, ('heads', 'sub'), scatter_dimension=1, til...  15.5 us
    all_gather x1, blocking collectives, per_device(): lax.all_gather(keys_own, 'blk', axis=0, tiled=True)  15.2 us
    all_gather x1, blocking collectives, per_device(): lax.all_gather(values_own, 'blk', axis=0, tiled=True)  14.4 us
    psum x1, blocking collectives, per_device(): conv_grad = lax.psum(conv_terms, 'blk') * norm  13.3 us
    ppermute x2, starting transfers between devices, padded(): lax.ppermute(tail, axis, [(i, (i + 1) % count) for i in range(ends)])  8.32 us
    all_gather x1, blocking collectives, per_device(): cot_full = lax.all_gather(cotangent, ('heads', 'sub'), axis=1, tiled=True)  6 us
  transfers between devices with their start and end apart: 9, of which 5 were waited for; matrix products, arithmetic and copies ran while one was open for 9% of the time, Pallas kernels for 0%

commit v1 on v0

--- a/solution.py
+++ b/solution.py
@@ -6,6 +6,19 @@
 D = 1024
 HEADS = 16
 TILE = 128
+
+
+def ring_gather(x, axis, dim):
+    ways = lax.axis_size(axis)
+    up = [(d, (d + 1) % ways) for d in range(ways)]
+    down = [(d, (d - 1) % ways) for d in range(ways)]
+    earlier, later = ([x], [x])
+    for _ in range(ways // 2):
+        earlier.append(lax.ppermute(earlier[-1], axis, up))
+    for _ in range((ways - 1) // 2):
+        later.append(lax.ppermute(later[-1], axis, down))
+    line = jnp.concatenate([*earlier[::-1], *later[1:]], axis=dim)
+    return jnp.roll(line, (lax.axis_index(axis) - ways // 2) * x.shape[dim], axis=dim)
 
 
 def padded(cells, sides, width):
@@ -65,7 +78,7 @@
     values_own = jnp.dot(mixed, w_value, preferred_element_type=jnp.float32).astype(jnp.bfloat16)
     keys_all, values_all = (
         lax.all_gather(keys_own, "blk", axis=0, tiled=True),
-        lax.all_gather(values_own, "blk", axis=0, tiled=True),
+        ring_gather(values_own, "blk", 0),
     )
     cot_full = lax.all_gather(cotangent, ("heads", "sub"), axis=1, tiled=True)
     grad_att = jnp.dot(cot_full, w_output, preferred_element_type=jnp.float32).astype(jnp.bfloat16)

time: 203 us -> 207 us (1.020)
  blocking collectives: 48.9 us -> 33.6 us
  local copies, waits for them, and re-layouts: 7.87 us -> 12.8 us
  starting transfers between devices: 13.7 us -> 17.8 us
  other arithmetic: 9.88 us -> 13.6 us
  waiting for transfers between devices: 92.5 us -> 95.7 us
  matrix products: 14.4 us -> 17.5 us
    all_gather x1 -> x0, blocking collectives: 14.4 us -> none  [per_device(): lax.all_gather(values_own, 'blk', axis=0, tiled=True)]
    ppermute x0 -> x3, starting transfers between devices: none -> 6.69 us  [the longest x1 4.72 us: ring_gather(): later.append(lax.ppermute(later[-1], axis, down))]
    ppermute x0 -> x3, waiting for transfers between devices: none -> 4.21 us  [the longest x2 4.21 us: ring_gather(): earlier.append(lax.ppermute(earlier[-1], axis, up))]
    ppermute x3, starting transfers between devices: 2.73 us -> 0.11 us  [from_behind(): return lax.ppermute(value, axis, pairs)]
    unnamed x10 -> x19, local copies, waits for them, and re-layouts: 0.03 us -> 2.59 us
    dynamic_slice x0 -> x2, local copies, waits for them, and re-layouts: none -> 2.52 us  [ring_gather(): jnp.roll(line, (lax.axis_index(axis) - ways // 2) * x.shape[dim], axis=dim)]
    add x3, other arithmetic: 0.09 us -> 2.19 us  [turn(): return (accum_q + query_add, moved + term)]
  transfers between devices with their start and end apart: 9 -> 12, of which waited for: 5 -> 6; matrix products, arithmetic and copies ran while one was open for 9% -> 11% of each run, Pallas kernels for 0% -> 0%
where the time goes in v1:
time: 207 us; the launch traced here: 206 us
  waiting for transfers between devices  95.7 us (46%)
  blocking collectives  33.6 us (16%)
  starting transfers between devices  17.8 us (9%)
  matrix products  17.5 us (8%)
  between operations  14.5 us (7%)
  other arithmetic  13.6 us (7%)
  local copies, waits for them, and re-layouts  12.8 us (6%)
    reduce_scatter x1, waiting for transfers between devices, per_device(): lax.psum_scatter(stacked, 'blk', scatter_dimension=1, tiled=True) * norm  58.1 us
    ppermute x3, waiting for transfers between devices, from_behind(): return lax.ppermute(value, axis, pairs)  17.7 us
    reduce_scatter x1, waiting for transfers between devices, per_device(): lax.psum_scatter(partial_grad, ('heads', 'sub'), scatter_dimension=1, til...  15.6 us
    all_gather x1, blocking collectives, per_device(): lax.all_gather(keys_own, 'blk', axis=0, tiled=True)  14.3 us
    psum x1, blocking collectives, per_device(): conv_grad = lax.psum(conv_terms, 'blk') * norm  13.3 us
    ppermute x2, starting transfers between devices, padded(): lax.ppermute(tail, axis, [(i, (i + 1) % count) for i in range(ends)])  8.34 us
    all_gather x1, blocking collectives, per_device(): cot_full = lax.all_gather(cotangent, ('heads', 'sub'), axis=1, tiled=True)  6 us
    ppermute x1, starting transfers between devices, ring_gather(): later.append(lax.ppermute(later[-1], axis, down))  4.72 us
  transfers between devices with their start and end apart: 12, of which 6 were waited for; matrix products, arithmetic and copies ran while one was open for 11% of the time, Pallas kernels for 0%

profile of v1, /device:TPU:0, one launch (start us, length us, event | category | flops | bytes accessed | tf_op | source)
XLA Modules:
  0.0 205.7 jit_solution(17939998910977129962)
XLA Ops:
  8.1 4.9 %collective-permute-start.1 = (bf16[1,1024]{1,0:T(2,128)(2,1)S(1)}, bf16[1,1024]{1,0:T(2,128)(2,1)S(1)}, u32[]{:S(2)}, u32[]{:S(2)}) collective-permute-start(bf16[1,1024]{1,0:T(2,128)(2,1)S(1)} %get-tuple-element.416), channel_id=1, source_target_pairs={{0,4},{4,8},{8,12},{1,5},{5,9},{9,13},{2,6},{6,10},{10,14},{3,7},{... | collective-permute-start | bytes 6152 | tf_op jit(solution)/shard_map/ppermute | solution.py:32
  13.0 1.3 collective-permute-start.2
  15.9 6.0 %all_gather.7 = bf16[128,1024]{1,0:T(8,128)(2,1)S(1)} all-gather(bf16[128,256]{1,0:T(8,128)(2,1)} %param.17), channel_id=1, replica_groups=mesh['groups'=2,'blk'=4,'heads'=2,'sub'=2] {'heads','sub'}, dimensions={1}, use_global_device_ids=true | all-gather | bytes 327680 | tf_op jit(solution)/shard_map/all_gather | solution.py:83
  22.2 1.0 convolution_compare_fusion.1
  23.1 1.3 convolution_convert_fusion.2
  24.8 1.0 maximum_convert_fusion
  26.3 4.7 %collective-permute-start.5 = (bf16[128,256]{1,0:T(8,128)(2,1)S(1)}, bf16[128,256]{1,0:T(8,128)(2,1)}, u32[]{:S(2)}, u32[]{:S(2)}) collective-permute-start(bf16[128,256]{1,0:T(8,128)(2,1)S(1)} %convolution_convert_fusion.1), channel_id=1, source_target_pairs={{0,12},{4,0},{8,4},{12,8},{1,13},{5,1},{9,5},{13,9},{2,14},{6,2},{... | collective-permute-start | bytes 196616 | tf_op jit(solution)/shard_map/ppermute | solution.py:19
  31.3 14.3 %all_gather.6 = bf16[512,256]{1,0:T(8,128)(2,1)S(1)} all-gather(bf16[128,256]{1,0:T(8,128)(2,1)S(1)} %convolution_convert_fusion.4), channel_id=1, replica_groups=mesh['groups'=2,'blk'=4,'heads'=2,'sub'=2] {'blk'}, dimensions={0}, use_global_device_ids=true | all-gather | bytes 327680 | tf_op jit(solution)/shard_map/all_gather | solution.py:80
  46.3 2.2 %fusion.50 = (f32[4,128]{1,0:T(4,128)S(1)}, bf16[4,128,512]{2,1,0:T(8,128)(2,1)}) fusion(bf16[128,4,64]{0,2,1:T(8,128)(2,1)S(1)} %bitcast.177, bf16[512,4,64]{0,2,1:T(8,128)(2,1)S(1)} %bitcast.181, pred[128,512]{1,0:T(8,128)(4,1)} %convolution_compare_fusion.1), kind=kOutput, calls=%fused_computation.135 | convolution fusion | flops 34864640 | bytes 919552 | tf_op jit(solution)/shard_map/while/body/eval_jaxpr/qhd,khd->hqk/dot_general | solution.py:99
  48.7 2.0 collective-permute-start.4
  50.8 4.2 %collective-permute-done.4 = bf16[128,256]{1,0:T(8,128)(2,1)S(1)} collective-permute-done((bf16[128,256]{1,0:T(8,128)(2,1)}, bf16[128,256]{1,0:T(8,128)(2,1)S(1)}, u32[]{:S(2)}, u32[]{:S(2)}) %collective-permute-start.4) | collective-permute-done | bytes 65568 | tf_op jit(solution)/shard_map/ppermute | solution.py:17
  59.2 1.8 copy.40
  61.7 2.1 %fusion.37 = (f32[4,128]{1,0:T(4,128)S(1)}, f32[4,128,64]{1,2,0:T(8,128)}) fusion(f32[4,128]{1,0:T(4,128)S(1)} %get-tuple-element.518, bf16[128,256]{0,1:T(8,128)(2,1)S(1)} %copy.38, bf16[512,4,64]{0,2,1:T(8,128)(2,1)} %bitcast.20, bf16[4,128,512]{2,1,0:T(8,128)(2,1)} %get-tuple-element.428), kind=kOutput, calls=%fused_computation.89 | convolution fusion | flops 33684992 | bytes 987136 | tf_op jit(solution)/shard_map/while/body/eval_jaxpr/hqk,khd->hqd/dot_general | solution.py:109
  63.8 1.1 fusion.24
  64.9 1.0 convolution_bitcast_fusion.5
  66.8 27.3 %while.23 = (s32[]{:T(128)}, f32[128,4,64]{0,2,1:T(8,128)S(1)}, f32[2,128,256]{1,2,0:T(8,128)}, s32[]{:T(128)}, bf16[512,256]{0,1:T(8,128)(2,1)S(1)}, /*index=5*...) while((s32[]{:T(128)}, f32[128,4,64]{0,2,1:T(8,128)S(1)}, ...), condition=%wide.region_2.3_spmd, body=%wide.region_1.2_spmd.sunk | while | flops 42853904 | bytes 4331956 | solution.py:170
  69.3 5.8 %collective-permute-done = f32[2,128,256]{1,2,0:T(8,128)S(1)} collective-permute-done((f32[2,128,256]{1,2,0:T(8,128)}, f32[2,128,256]{1,2,0:T(8,128)S(1)}, u32[]{:S(2)}, u32[]{:S(2)}) %collective-permute-start) | collective-permute-done | bytes 262176 | tf_op jit(solution)/shard_map/while/body/eval_jaxpr/ppermute | solution.py:44
  78.3 5.9 %collective-permute-done = f32[2,128,256]{1,2,0:T(8,128)S(1)} collective-permute-done((f32[2,128,256]{1,2,0:T(8,128)}, f32[2,128,256]{1,2,0:T(8,128)S(1)}, u32[]{:S(2)}, u32[]{:S(2)}) %collective-permute-start) | collective-permute-done | bytes 262176 | tf_op jit(solution)/shard_map/while/body/eval_jaxpr/ppermute | solution.py:44
  87.5 5.9 %collective-permute-done = f32[2,128,256]{1,2,0:T(8,128)S(1)} collective-permute-done((f32[2,128,256]{1,2,0:T(8,128)}, f32[2,128,256]{1,2,0:T(8,128)S(1)}, u32[]{:S(2)}, u32[]{:S(2)}) %collective-permute-start) | collective-permute-done | bytes 262176 | tf_op jit(solution)/shard_map/while/body/eval_jaxpr/ppermute | solution.py:44
  94.1 1.0 convert.4
  95.8 1.1 convolution_add_fusion
  98.3 2.2 %pad_maximum_fusion = f32[4,1024,256]{2,1,0:T(8,128)} fusion(f32[1,1024,256]{2,1,0:T(8,128)S(1)} %convolution_bitcast_fusion.1, f32[1,1024,256]{2,1,0:T(8,128)S(1)} %convolution_bitcast_fusion.2, f32[1,1024,256]{2,1,0:T(8,128)S(1)} %convolution_bitcast_fusion.3, f32[1,1024,256]{2,1,0:T(8,128)S(1)} %convolution_bitcast_fusion.4), kind=kLoop, calls=%fused_computation.32 | loop fusion | flops 3145728 | bytes 8388608 | tf_op jit(solution)/shard_map/stack | solution.py:174
  100.6 0.9 dynamic-slice_add_fusion
  101.5 15.6 %reduce-scatter.3.cloned.1.call-done = f32[128,256]{1,0:T(8,128)} async-done(((f32[128,1024]{1,0:T(8,128)}), f32[128,256]{1,0:T(8,128)}) %reduce-scatter.3.cloned.1.call-update) | async-done | bytes 131088 | tf_op jit(solution)/shard_map/reduce_scatter | solution.py:188
  117.0 1.1 fusion.33
  118.1 3.4 %collective-permute-start.6 = (bf16[1,256]{1,0:T(2,128)(2,1)S(1)}, bf16[1,256]{1,0:T(2,128)(2,1)S(1)}, u32[]{:S(2)}, u32[]{:S(2)}) collective-permute-start(bf16[1,256]{1,0:T(2,128)(2,1)S(1)} %get-tuple-element.419), channel_id=1, source_target_pairs={{0,4},{4,8},{8,12},{1,5},{5,9},{9,13},{2,6},{6,10},{10,14},{3,7},{... | collective-permute-start | bytes 1544 | tf_op jit(solution)/shard_map/ppermute | solution.py:32
  121.5 1.3 collective-permute-start.7
  122.8 13.3 %psum.7 = f32[3,256]{1,0:T(4,128)S(1)} all-reduce(f32[3,256]{1,0:T(4,128)S(1)} %pad_maximum_fusion.2), channel_id=1, replica_groups=mesh['groups'=2,'blk'=4,'heads'=2,'sub'=2] {'blk'}, use_global_device_ids=true, to_apply=%region_7.8 | all-reduce | flops 768 | bytes 6144 | tf_op jit(solution)/shard_map/psum | solution.py:208
  136.7 1.6 fusion.34
  138.4 58.1 %reduce-scatter.5.cloned.1.call-done = f32[4,256,256]{2,1,0:T(8,128)} async-done(((f32[4,1024,256]{2,1,0:T(8,128)}), f32[4,256,256]{2,1,0:T(8,128)}) %reduce-scatter.5.cloned.1.call-update) | async-done | bytes 1048592 | tf_op jit(solution)/shard_map/reduce_scatter | solution.py:182
  196.5 1.3 broadcast_multiply_fusion
  197.8 1.0 slice_bitcast_fusion
  (103 shorter events, 22.6 us)
Async XLA Ops:
  7.2 38.6 %copy-start = (bf16[1024,256]{1,0:T(8,128)(2,1)S(1)}, bf16[1024,256]{1,0:T(8,128)(2,1)}, u32[]{:S(2)}) copy-start(bf16[1024,256]{1,0:T(8,128)(2,1)} %param.12) | copy-start | bytes 1572868
  7.2 18.9 %copy-start.2 = (bf16[1024,256]{1,0:T(8,128)(2,1)S(1)}, bf16[1024,256]{1,0:T(8,128)(2,1)}, u32[]{:S(2)}) copy-start(bf16[1024,256]{1,0:T(8,128)(2,1)} %param.14) | copy-start | bytes 1572868
  7.2 23.8 %copy-start.1 = (bf16[1024,256]{1,0:T(8,128)(2,1)S(1)}, bf16[1024,256]{1,0:T(8,128)(2,1)}, u32[]{:S(2)}) copy-start(bf16[1024,256]{1,0:T(8,128)(2,1)} %param.13) | copy-start | bytes 1572868
  7.2 109.8 %reduce-scatter.3.cloned.1.call-start = ((), (), s32[]{:S(2)}) async-start(), calls=%async_computation.2 | async-start | bytes 655360 | tf_op jit(solution)/shard_map/reduce_scatter | solution.py:188
  8.1 16.7 %collective-permute-start.1 = (bf16[1,1024]{1,0:T(2,128)(2,1)S(1)}, bf16[1,1024]{1,0:T(2,128)(2,1)S(1)}, u32[]{:S(2)}, u32[]{:S(2)}) collective-permute-start(bf16[1,1024]{1,0:T(2,128)(2,1)S(1)} %get-tuple-element.416), channel_id=1, source_target_pairs={{0,4},{4,8},{8,12},{1,5},{5,9},{9,13},{2,6},{6,10},{10,14},{3,7},{... | collective-permute-start | bytes 6152 | tf_op jit(solution)/shard_map/ppermute | solution.py:32
  13.0 11.8 %collective-permute-start.2 = (bf16[1,1024]{1,0:T(2,128)(2,1)S(1)}, bf16[1,1024]{1,0:T(2,128)(2,1)S(1)}, u32[]{:S(2)}, u32[]{:S(2)}) collective-permute-start(bf16[1,1024]{1,0:T(2,128)(2,1)S(1)} %get-tuple-element.417), channel_id=1, source_target_pairs={{4,0},{8,4},{12,8},{5,1},{9,5},{13,9},{6,2},{10,6},{14,10},{7,3},{... | collective-permute-start | bytes 6152 | tf_op jit(solution)/shard_map/ppermute | solution.py:34
  26.3 29.6 %collective-permute-start.5 = (bf16[128,256]{1,0:T(8,128)(2,1)S(1)}, bf16[128,256]{1,0:T(8,128)(2,1)}, u32[]{:S(2)}, u32[]{:S(2)}) collective-permute-start(bf16[128,256]{1,0:T(8,128)(2,1)S(1)} %convolution_convert_fusion.1), channel_id=1, source_target_pairs={{0,12},{4,0},{8,4},{12,8},{1,13},{5,1},{9,5},{13,9},{2,14},{6,2},{... | collective-permute-start | bytes 196616 | tf_op jit(solution)/shard_map/ppermute | solution.py:19
  31.0 17.7 %collective-permute-start.3 = (bf16[128,256]{1,0:T(8,128)(2,1)S(1)}, bf16[128,256]{1,0:T(8,128)(2,1)}, u32[]{:S(2)}, u32[]{:S(2)}) collective-permute-start(bf16[128,256]{1,0:T(8,128)(2,1)S(1)} %convolution_convert_fusion.1), channel_id=1, source_target_pairs={{0,4},{4,8},{8,12},{12,0},{1,5},{5,9},{9,13},{13,1},{2,6},{6,10},{... | collective-permute-start | bytes 196616 | tf_op jit(solution)/shard_map/ppermute | solution.py:17
  46.2 4.4 %copy-start.4 = (bf16[128,256]{0,1:T(8,128)(2,1)}, bf16[128,256]{0,1:T(8,128)(2,1)S(1)}, u32[]{:S(2)}) copy-start(bf16[128,256]{0,1:T(8,128)(2,1)S(1)} %copy.35) | copy-start | bytes 196612
  48.7 6.3 %collective-permute-start.4 = (bf16[128,256]{1,0:T(8,128)(2,1)}, bf16[128,256]{1,0:T(8,128)(2,1)S(1)}, u32[]{:S(2)}, u32[]{:S(2)}) collective-permute-start(bf16[128,256]{1,0:T(8,128)(2,1)} %collective-permute-done.3), channel_id=1, source_target_pairs={{0,4},{4,8},{8,12},{12,0},{1,5},{5,9},{9,13},{13,1},{2,6},{6,10},{... | collective-permute-start | bytes 196616 | tf_op jit(solution)/shard_map/ppermute | solution.py:17
  66.8 8.4 %collective-permute-start = (f32[2,128,256]{1,2,0:T(8,128)}, f32[2,128,256]{1,2,0:T(8,128)S(1)}, u32[]{:S(2)}, u32[]{:S(2)}) collective-permute-start(f32[2,128,256]{1,2,0:T(8,128)} %get-tuple-element.531), channel_id=1, source_target_pairs={{0,4},{4,8},{8,12},{12,0},{1,5},{5,9},{9,13},{13,1},{2,6},{6,10},{... | collective-permute-start | bytes 786440 | tf_op jit(solution)/shard_map/while/body/eval_jaxpr/ppermute | solution.py:44
  75.9 8.4 %collective-permute-start = (f32[2,128,256]{1,2,0:T(8,128)}, f32[2,128,256]{1,2,0:T(8,128)S(1)}, u32[]{:S(2)}, u32[]{:S(2)}) collective-permute-start(f32[2,128,256]{1,2,0:T(8,128)} %get-tuple-element.531), channel_id=1, source_target_pairs={{0,4},{4,8},{8,12},{12,0},{1,5},{5,9},{9,13},{13,1},{2,6},{6,10},{... | collective-permute-start | bytes 786440 | tf_op jit(solution)/shard_map/while/body/eval_jaxpr/ppermute | solution.py:44
  85.0 8.4 %collective-permute-start = (f32[2,128,256]{1,2,0:T(8,128)}, f32[2,128,256]{1,2,0:T(8,128)S(1)}, u32[]{:S(2)}, u32[]{:S(2)}) collective-permute-start(f32[2,128,256]{1,2,0:T(8,128)} %get-tuple-element.531), channel_id=1, source_target_pairs={{0,4},{4,8},{8,12},{12,0},{1,5},{5,9},{9,13},{13,1},{2,6},{6,10},{... | collective-permute-start | bytes 786440 | tf_op jit(solution)/shard_map/while/body/eval_jaxpr/ppermute | solution.py:44
  95.4 2.5 %copy-start.5 = (f32[4,128,64]{1,2,0:T(8,128)S(1)}, f32[4,128,64]{1,2,0:T(8,128)}, u32[]{:S(2)}) copy-start(f32[4,128,64]{1,2,0:T(8,128)} %get-tuple-element.430) | copy-start | bytes 393220
  96.9 99.6 %reduce-scatter.5.cloned.1.call-start = ((), (), s32[]{:S(2)}) async-start(), calls=%async_computation.3 | async-start | bytes 5242880 | tf_op jit(solution)/shard_map/reduce_scatter | solution.py:182
  100.5 16.5 %copy-start.3 = (bf16[128,256]{1,0:T(8,128)(2,1)S(1)}, bf16[128,256]{1,0:T(8,128)(2,1)}, u32[]{:S(2)}) copy-start(bf16[128,256]{1,0:T(8,128)(2,1)} %param.17) | copy-start | bytes 196612
  118.1 18.6 %collective-permute-start.6 = (bf16[1,256]{1,0:T(2,128)(2,1)S(1)}, bf16[1,256]{1,0:T(2,128)(2,1)S(1)}, u32[]{:S(2)}, u32[]{:S(2)}) collective-permute-start(bf16[1,256]{1,0:T(2,128)(2,1)S(1)} %get-tuple-element.419), channel_id=1, source_target_pairs={{0,4},{4,8},{8,12},{1,5},{5,9},{9,13},{2,6},{6,10},{10,14},{3,7},{... | collective-permute-start | bytes 1544 | tf_op jit(solution)/shard_map/ppermute | solution.py:32
  121.5 15.2 %collective-permute-start.7 = (bf16[1,256]{1,0:T(2,128)(2,1)S(1)}, bf16[1,256]{1,0:T(2,128)(2,1)S(1)}, u32[]{:S(2)}, u32[]{:S(2)}) collective-permute-start(bf16[1,256]{1,0:T(2,128)(2,1)S(1)} %get-tuple-element.420), channel_id=1, source_target_pairs={{4,0},{8,4},{12,8},{5,1},{9,5},{13,9},{6,2},{10,6},{14,10},{7,3},{... | collective-permute-start | bytes 1544 | tf_op jit(solution)/shard_map/ppermute | solution.py:34
Sparse Core Ops, SparseCore 0:
  97.0 19.9 reduce-scatter.2
  119.4 77.0 reduce-scatter.4
